TPU v7x, 512 devices: a whole 4x4x16 slice. The times are simulated.
512 devices in a mesh: tm: 32 (over z, core), space: 16 (over x, y).
Axes of the slice: x: 4, y: 4, z: 16, core: 2. Of those that a mesh axis runs over, the one named last changes fastest.
Arguments:
- snapshots: bfloat16 [16384, 4096], P('space', 'tm'), may hold values from -23 to 23
- energy: bfloat16 [128, 7, 128, 128], P('space'), may hold values from -0.375 to 0.375
- neighbours: int32 [128, 7], P('space'), may hold values from 0 to 127, as said below
- sketch: float32 [5, 256, 128], replicated, may hold values from -0.375 to 0.375
Outputs:
- modes: bfloat16 [6, 32, 16384, 128], P(None, 'tm', 'space')
Inputs may be any that keep to these rules, and one draw needn't show every extreme that they name: `neighbours`: entry [b, k] lies within 2 blocks of b.
All inputs are finite; a program needn't handle non-finite values.
Results may differ from a plain program's by a relative error of at most 0.017.
Values may be sent and summed in bfloat16 or wider, within the bound.
A program may use at most 64 MiB of HBM per device.

v0:
```python
import jax
import jax.numpy as jnp
from jax import lax
from jax.sharding import PartitionSpec as P

HB = 2


def padded_2(cells, sides, width):
    for axis, dim in sides:
        count = lax.axis_size(axis)
        ends = count - 1
        head = lax.slice_in_dim(cells, 0, width, axis=dim)
        tail = lax.slice_in_dim(cells, cells.shape[dim] - width, cells.shape[dim], axis=dim)
        cells = jnp.concatenate(
            [
                lax.ppermute(tail, axis, [(i, (i + 1) % count) for i in range(ends)]),
                cells,
                lax.ppermute(head, axis, [((i + 1) % count, i) for i in range(ends)]),
            ],
            axis=dim,
        )
    return cells


def from_partner(value, axis, bit):
    mask = 2**bit
    pairs = [(source, source ^ mask) for source in range(lax.axis_size(axis))]
    return lax.ppermute(value, axis, pairs)


def blocked(matrix_rows, block_rows):
    return matrix_rows.reshape(matrix_rows.shape[0] // block_rows, block_rows, matrix_rows.shape[1])


def image_of(padded, source, energy, local_index):
    block_rows = energy.shape[2]
    running = 3.0 * blocked(source, block_rows).astype(jnp.float32)
    for slot_index in range(energy.shape[1]):
        gathered = jnp.take(padded, local_index[:, slot_index], axis=0)
        running = running + jnp.einsum(
            "nij,njw->niw", energy[:, slot_index], gathered, preferred_element_type=jnp.float32
        )
    return running.astype(jnp.bfloat16).reshape(source.shape[0], source.shape[1])


def gram_of(energy_image):
    return jnp.einsum("rc,rd->cd", energy_image, energy_image, preferred_element_type=jnp.float32)


def side_by_side(upper_half, first, second, axis_number):
    return jnp.where(
        upper_half,
        jnp.concatenate([second, first], axis_number),
        jnp.concatenate([first, second], axis_number),
    )


def on_device(snapshots, energy, neighbours, sketch):
    block_rows = energy.shape[2]
    block_count = energy.shape[0]
    rows_dev = snapshots.shape[0]
    total_rows = rows_dev * lax.axis_size("space")
    first_block = lax.axis_index("space") * block_count - HB
    local_index = neighbours - first_block
    window_index = lax.axis_index("tm")
    highest = lax.Precision.HIGHEST
    padded = padded_2(blocked(snapshots, block_rows), (("space", 0),), HB)
    energy_image = image_of(padded, snapshots, energy, local_index)
    gram_matrix = lax.psum(gram_of(energy_image), "space") / total_rows
    lower_factor = jnp.linalg.cholesky(gram_matrix)
    identity = jnp.eye(snapshots.shape[1], dtype=jnp.float32)
    coefficients = jax.scipy.linalg.solve_triangular(lower_factor, identity, lower=True).T.astype(
        jnp.bfloat16
    )
    current = jnp.dot(snapshots, coefficients, preferred_element_type=jnp.float32).astype(
        jnp.bfloat16
    )
    images = jnp.dot(energy_image, coefficients, preferred_element_type=jnp.float32).astype(
        jnp.bfloat16
    )
    levels_kept = [current]
    for tree_level in range(sketch.shape[0]):
        upper_half = window_index // 2**tree_level % 2 == 1
        partner, partner_image = from_partner((current, images), "tm", tree_level)
        joined = side_by_side(upper_half, current, partner, 1)
        joined_image = side_by_side(upper_half, images, partner_image, 1)
        sketch_level = sketch[tree_level]
        gram_matrix = lax.psum(gram_of(joined_image), "space") / total_rows
        columns = jnp.dot(gram_matrix, sketch_level, precision=highest)
        inner_gram = jnp.dot(
            columns.T, jnp.dot(gram_matrix, columns, precision=highest), precision=highest
        )
        lower_factor = jnp.linalg.cholesky(inner_gram)
        coefficients = jax.scipy.linalg.solve_triangular(
            lower_factor, columns.T, lower=True
        ).T.astype(jnp.bfloat16)
        new_modes = jnp.dot(joined, coefficients, preferred_element_type=jnp.float32).astype(
            jnp.bfloat16
        )
        new_image = jnp.dot(joined_image, coefficients, preferred_element_type=jnp.float32).astype(
            jnp.bfloat16
        )
        current = new_modes
        images = new_image
        levels_kept.append(current)
    return jnp.stack(levels_kept)[:, None]


def solution(mesh):
    placed = (P("space", "tm"), P("space", None, None, None), P("space", None), P())
    return jax.shard_map(
        on_device,
        mesh=mesh,
        in_specs=placed,
        out_specs=P(None, "tm", "space", None),
        check_vma=False,
    )
```

profile of v0, /device:TPU:1, one launch (start us, length us, event | category | flops | bytes accessed | tf_op | source)
XLA Modules:
  0.0 996.7 jit_solution(3480264746523409155)
XLA Ops:
  8.7 4.7 collective-permute-start
  28.0 118.8 %all-reduce.7.cloned.1.call-done = f32[128,128]{0,1:T(8,128)} async-done(((f32[128,128]{0,1:T(8,128)}), f32[128,128]{0,1:T(8,128)}) %all-reduce.7.cloned.1.call-update) | async-done | bytes 65552 | tf_op jit(solution)/shard_map/psum | solution.py:70
  148.6 11.7 %cholesky.104 = f32[128,128]{1,0:T(8,128)S(1)} custom-call(f32[128,128]{1,0:T(8,128)S(1)} %fusion.148), custom_call_target="Cholesky" | custom-call | tf_op jit(solution)/shard_map/jit(cholesky)/cholesky | solution.py:71
  161.7 9.8 custom-call.9
  172.1 4.1 collective-permute-start.3
  178.7 112.8 %all-reduce.9.cloned.1.call-done = f32[256,256]{1,0:T(8,128)} async-done(((f32[256,256]{1,0:T(8,128)}), f32[256,256]{1,0:T(8,128)}) %all-reduce.9.cloned.1.call-update) | async-done | bytes 262160 | tf_op jit(solution)/shard_map/psum | solution.py:89
  291.6 1.3 fusion.93
  292.9 1.3 fusion.91
  294.7 11.7 %cholesky.115 = f32[128,128]{1,0:T(8,128)S(1)} custom-call(f32[128,128]{1,0:T(8,128)S(1)} %fusion.146), custom_call_target="Cholesky" | custom-call | tf_op jit(solution)/shard_map/jit(cholesky)/cholesky | solution.py:94
  307.8 9.8 custom-call.14
  318.2 3.2 collective-permute-start.5
  321.4 4.5 collective-permute-done.5
  327.4 114.8 %all-reduce.11.cloned.1.call-done = f32[256,256]{1,0:T(8,128)} async-done(((f32[256,256]{1,0:T(8,128)}), f32[256,256]{1,0:T(8,128)}) %all-reduce.11.cloned.1.call-update) | async-done | bytes 262160 | tf_op jit(solution)/shard_map/psum | solution.py:89
  442.2 1.3 fusion.89
  443.6 1.3 fusion.87
  445.4 11.7 %cholesky.126 = f32[128,128]{1,0:T(8,128)S(1)} custom-call(f32[128,128]{1,0:T(8,128)S(1)} %fusion.144), custom_call_target="Cholesky" | custom-call | tf_op jit(solution)/shard_map/jit(cholesky)/cholesky | solution.py:94
  458.5 9.8 custom-call.15
  468.9 4.2 collective-permute-start.7
  473.1 11.4 %collective-permute-done.7 = bf16[1024,128]{0,1:T(8,128)(2,1)S(1)} collective-permute-done((bf16[1024,128]{0,1:T(8,128)(2,1)S(1)}, bf16[1024,128]{0,1:T(8,128)(2,1)S(1)}, u32[]{:S(2)}, u32[]{:S(2)}) %collective-permute-start.7) | collective-permute-done | bytes 262176 | tf_op jit(solution)/shard_map/ppermute | solution.py:29
  485.9 3.9 collective-permute-start.2
  489.9 109.4 %all-reduce.13.cloned.1.call-done = f32[256,256]{1,0:T(8,128)} async-done(((f32[256,256]{1,0:T(8,128)}), f32[256,256]{1,0:T(8,128)}) %all-reduce.13.cloned.1.call-update) | async-done | bytes 262160 | tf_op jit(solution)/shard_map/psum | solution.py:89
  599.3 1.3 fusion.85
  600.6 1.3 fusion.83
  602.4 11.7 %cholesky.137 = f32[128,128]{1,0:T(8,128)S(1)} custom-call(f32[128,128]{1,0:T(8,128)S(1)} %fusion.142), custom_call_target="Cholesky" | custom-call | tf_op jit(solution)/shard_map/jit(cholesky)/cholesky | solution.py:94
  615.5 9.8 custom-call.16
  625.6 1.3 convolution_convert_fusion.3
  627.0 7.4 collective-permute-start.9
  634.4 1.3 bitcast_dynamic-update-slice_fusion.4
  635.7 3.2 collective-permute-start.4
  638.9 18.0 %collective-permute-done.9 = bf16[1024,128]{0,1:T(8,128)(2,1)S(1)} collective-permute-done((bf16[1024,128]{0,1:T(8,128)(2,1)S(1)}, bf16[1024,128]{0,1:T(8,128)(2,1)S(1)}, u32[]{:S(2)}, u32[]{:S(2)}) %collective-permute-start.9) | collective-permute-done | bytes 262176 | tf_op jit(solution)/shard_map/ppermute | solution.py:29
  659.1 4.3 collective-permute-start.6
  663.5 108.2 %all-reduce.15.cloned.1.call-done = f32[256,256]{1,0:T(8,128)} async-done(((f32[256,256]{1,0:T(8,128)}), f32[256,256]{1,0:T(8,128)}) %all-reduce.15.cloned.1.call-update) | async-done | bytes 262160 | tf_op jit(solution)/shard_map/psum | solution.py:89
  771.7 1.3 fusion.81
  773.0 1.3 fusion.79
  774.8 11.7 %cholesky.148 = f32[128,128]{1,0:T(8,128)S(1)} custom-call(f32[128,128]{1,0:T(8,128)S(1)} %fusion.140), custom_call_target="Cholesky" | custom-call | tf_op jit(solution)/shard_map/jit(cholesky)/cholesky | solution.py:94
  787.9 9.8 custom-call.17
  799.0 12.5 %collective-permute-start.11 = (bf16[1024,128]{0,1:T(8,128)(2,1)}, bf16[1024,128]{0,1:T(8,128)(2,1)S(1)}, u32[]{:S(2)}, u32[]{:S(2)}) collective-permute-start(bf16[1024,128]{0,1:T(8,128)(2,1)} %convolution_convert_fusion.1), channel_id=1, source_target_pairs={{0,256},{16,272},{32,288},{48,304},{64,320},{80,336},{96,352},{112... | collective-permute-start | bytes 786440 | tf_op jit(solution)/shard_map/ppermute | solution.py:29
  811.6 1.5 bitcast_dynamic-update-slice_fusion.2
  813.1 2.6 collective-permute-start.8
  816.4 2.4 fusion.30
  818.9 39.5 %collective-permute-done.8 = bf16[1024,128]{0,1:T(8,128)(2,1)S(1)} collective-permute-done((bf16[1024,128]{0,1:T(8,128)(2,1)S(1)}, bf16[1024,128]{0,1:T(8,128)(2,1)S(1)}, u32[]{:S(2)}, u32[]{:S(2)}) %collective-permute-start.8) | collective-permute-done | bytes 262176 | tf_op jit(solution)/shard_map/ppermute | solution.py:29
  858.8 7.6 collective-permute-start.10
  866.3 95.1 %all-reduce.17.cloned.1.call-done = f32[256,256]{1,0:T(8,128)} async-done(((f32[256,256]{1,0:T(8,128)}), f32[256,256]{1,0:T(8,128)}) %all-reduce.17.cloned.1.call-update) | async-done | bytes 262160 | tf_op jit(solution)/shard_map/psum | solution.py:89
  961.4 1.3 fusion.77
  962.8 1.3 fusion.75
  964.6 11.7 %cholesky.159 = f32[128,128]{1,0:T(8,128)S(1)} custom-call(f32[128,128]{1,0:T(8,128)S(1)} %fusion.138), custom_call_target="Cholesky" | custom-call | tf_op jit(solution)/shard_map/jit(cholesky)/cholesky | solution.py:94
  977.6 9.8 custom-call.18
  988.1 1.6 copy.21
  (117 shorter events, 41.4 us)
Async XLA Ops:
  6.5 140.3 %all-reduce.7.cloned.1.call-start = ((), (), s32[]{:S(2)}) async-start(), calls=%async_computation | async-start | bytes 131072 | tf_op jit(solution)/shard_map/psum | solution.py:70
  7.4 7.1 collective-permute-start.1
  8.7 6.0 collective-permute-start
  16.3 5.7 copy-start.1
  25.7 1.0 copy-start
  28.0 263.6 %all-reduce.9.cloned.1.call-start = ((), (), s32[]{:S(2)}) async-start(), calls=%async_computation.1 | async-start | bytes 524288 | tf_op jit(solution)/shard_map/psum | solution.py:89
  171.8 119.8 %copy-start.2 = (f32[5,256,128]{2,1,0:T(8,128)S(1)}, f32[5,256,128]{2,1,0:T(8,128)}, u32[]{:S(2)}) copy-start(f32[5,256,128]{2,1,0:T(8,128)} %param.12) | copy-start | bytes 1966084
  172.1 5.3 collective-permute-start.3
  178.5 263.8 %all-reduce.11.cloned.1.call-start = ((), (), s32[]{:S(2)}) async-start(), calls=%async_computation.2 | async-start | bytes 524288 | tf_op jit(solution)/shard_map/psum | solution.py:89
  318.2 7.8 collective-permute-start.5
  327.1 272.2 %all-reduce.13.cloned.1.call-start = ((), (), s32[]{:S(2)}) async-start(), calls=%async_computation.3 | async-start | bytes 524288 | tf_op jit(solution)/shard_map/psum | solution.py:89
  468.9 15.6 %collective-permute-start.7 = (bf16[1024,128]{0,1:T(8,128)(2,1)S(1)}, bf16[1024,128]{0,1:T(8,128)(2,1)S(1)}, u32[]{:S(2)}, u32[]{:S(2)}) collective-permute-start(bf16[1024,128]{0,1:T(8,128)(2,1)S(1)} %convolution_convert_fusion.5), channel_id=1, source_target_pairs={{0,64},{16,80},{32,96},{48,112},{64,0},{80,16},{96,32},{112,48},{1... | collective-permute-start | bytes 786440 | tf_op jit(solution)/shard_map/ppermute | solution.py:29
  484.5 1.4 copy-start.3
  485.6 286.0 %all-reduce.15.cloned.1.call-start = ((), (), s32[]{:S(2)}) async-start(), calls=%async_computation.4 | async-start | bytes 524288 | tf_op jit(solution)/shard_map/psum | solution.py:89
  485.9 148.4 %collective-permute-start.2 = (bf16[1024,128]{0,1:T(8,128)(2,1)S(1)}, bf16[1024,128]{0,1:T(8,128)(2,1)}, u32[]{:S(2)}, u32[]{:S(2)}) collective-permute-start(bf16[1024,128]{0,1:T(8,128)(2,1)S(1)} %bitcast.206), channel_id=1, source_target_pairs={{0,16},{16,0},{32,48},{48,32},{64,80},{80,64},{96,112},{112,96},{1... | collective-permute-start | bytes 786440 | tf_op jit(solution)/shard_map/ppermute | solution.py:29
  627.0 30.0 %collective-permute-start.9 = (bf16[1024,128]{0,1:T(8,128)(2,1)S(1)}, bf16[1024,128]{0,1:T(8,128)(2,1)S(1)}, u32[]{:S(2)}, u32[]{:S(2)}) collective-permute-start(bf16[1024,128]{0,1:T(8,128)(2,1)S(1)} %convolution_convert_fusion.3), channel_id=1, source_target_pairs={{0,128},{16,144},{32,160},{48,176},{64,192},{80,208},{96,224},{112... | collective-permute-start | bytes 786440 | tf_op jit(solution)/shard_map/ppermute | solution.py:29
  635.7 22.4 %collective-permute-start.4 = (bf16[1024,128]{0,1:T(8,128)(2,1)S(1)}, bf16[1024,128]{0,1:T(8,128)(2,1)S(1)}, u32[]{:S(2)}, u32[]{:S(2)}) collective-permute-start(bf16[1024,128]{0,1:T(8,128)(2,1)S(1)} %get-tuple-element.20), channel_id=1, source_target_pairs={{0,32},{16,48},{32,0},{48,16},{64,96},{80,112},{96,64},{112,80},{1... | collective-permute-start | bytes 786440 | tf_op jit(solution)/shard_map/ppermute | solution.py:29
  658.1 303.4 %all-reduce.17.cloned.1.call-start = ((), (), s32[]{:S(2)}) async-start(), calls=%async_computation.5 | async-start | bytes 524288 | tf_op jit(solution)/shard_map/psum | solution.py:89
  659.1 152.4 %collective-permute-start.6 = (bf16[1024,128]{0,1:T(8,128)(2,1)}, bf16[1024,128]{0,1:T(8,128)(2,1)}, u32[]{:S(2)}, u32[]{:S(2)}) collective-permute-start(bf16[1024,128]{0,1:T(8,128)(2,1)} %get-tuple-element.22), channel_id=1, source_target_pairs={{0,64},{16,80},{32,96},{48,112},{64,0},{80,16},{96,32},{112,48},{1... | collective-permute-start | bytes 786440 | tf_op jit(solution)/shard_map/ppermute | solution.py:29
  799.0 17.4 %collective-permute-start.11 = (bf16[1024,128]{0,1:T(8,128)(2,1)}, bf16[1024,128]{0,1:T(8,128)(2,1)S(1)}, u32[]{:S(2)}, u32[]{:S(2)}) collective-permute-start(bf16[1024,128]{0,1:T(8,128)(2,1)} %convolution_convert_fusion.1), channel_id=1, source_target_pairs={{0,256},{16,272},{32,288},{48,304},{64,320},{80,336},{96,352},{112... | collective-permute-start | bytes 786440 | tf_op jit(solution)/shard_map/ppermute | solution.py:29
  813.1 45.4 %collective-permute-start.8 = (bf16[1024,128]{0,1:T(8,128)(2,1)S(1)}, bf16[1024,128]{0,1:T(8,128)(2,1)S(1)}, u32[]{:S(2)}, u32[]{:S(2)}) collective-permute-start(bf16[1024,128]{0,1:T(8,128)(2,1)S(1)} %get-tuple-element.24), channel_id=1, source_target_pairs={{0,128},{16,144},{32,160},{48,176},{64,192},{80,208},{96,224},{112... | collective-permute-start | bytes 786440 | tf_op jit(solution)/shard_map/ppermute | solution.py:29
  858.8 129.0 %collective-permute-start.10 = (bf16[1024,128]{0,1:T(8,128)(2,1)S(1)}, bf16[1024,128]{0,1:T(8,128)(2,1)S(1)}, u32[]{:S(2)}, u32[]{:S(2)}) collective-permute-start(bf16[1024,128]{0,1:T(8,128)(2,1)S(1)} %get-tuple-element.26), channel_id=1, source_target_pairs={{0,256},{16,272},{32,288},{48,304},{64,320},{80,336},{96,352},{112... | collective-permute-start | bytes 786440 | tf_op jit(solution)/shard_map/ppermute | solution.py:29
Sparse Core Ops, SparseCore 0:
  28.1 118.6 all-reduce.6
  178.6 112.9 all-reduce.8
  327.2 114.9 all-reduce.10
  485.7 113.4 all-reduce.12
  658.2 113.4 all-reduce.14
  819.0 142.3 all-reduce.16
where the time goes:
time: 1000 us; the launch traced here: 997 us
  waiting for transfers between devices  735 us (74%)
  other arithmetic  141 us (14%)
  starting transfers between devices  59.5 us (6%)
  matrix products  37.6 us (4%)
  between operations  14.6 us (1%)
    psum x5, waiting for transfers between devices, on_device(): gram_matrix = lax.psum(gram_of(joined_image), 'space') / total_rows  540 us
    psum x1, waiting for transfers between devices, on_device(): gram_matrix = lax.psum(gram_of(energy_image), 'space') / total_rows  119 us
    ppermute x10, waiting for transfers between devices, from_partner(): return lax.ppermute(value, axis, pairs)  75.4 us
    another operation x15, other arithmetic, on_device(): lower_factor = jnp.linalg.cholesky(inner_gram)  62 us
    ppermute x10, starting transfers between devices, from_partner(): return lax.ppermute(value, axis, pairs)  52.9 us
    another operation x10, other arithmetic, on_device(): jax.scipy.linalg.solve_triangular(lower_factor, columns.T, lower=True)  52.3 us
  transfers between devices with their start and end apart: 18, of which 13 were waited for; matrix products, arithmetic and copies ran while one was open for 9% of the time, Pallas kernels for 0%

commit v1 on v0

v1 whole, which is shorter than its diff:
```python
import functools

import jax
import jax.numpy as jnp
from jax import lax
from jax.experimental import pallas as pl
from jax.experimental.pallas import tpu as pltpu
from jax.sharding import PartitionSpec as P

K = 128
HB = 2
F32 = jnp.float32
BF16 = jnp.bfloat16
NN = ((1,), (0,))
NT = ((1,), (1,))
TN = ((0,), (0,))


def mm(a, b, dims=NN):
    return lax.dot_general(a, b, (dims, ((), ())), preferred_element_type=F32)


def split(a):
    high = a.astype(BF16)
    return high, (a - high.astype(F32)).astype(BF16)


def mm3(a, b, dims=NN):
    ah, al = split(a)
    bh, bl = split(b)
    return mm(ah, bh, dims) + (mm(ah, bl, dims) + mm(al, bh, dims))


def eliminate(t, n, nb):
    done = []
    for k0 in range(0, n, nb):
        rows = lax.broadcasted_iota(jnp.int32, t.shape, 0)
        cols = [jnp.broadcast_to(t[:, k0 + j : k0 + j + 1], t.shape) for j in range(nb)]
        for j in range(nb):
            pivot = 1.0 / cols[j][j : j + 1, :]
            factor = jnp.where(rows > j, cols[j] * pivot, 0.0)
            for i in range(j + 1, nb):
                cols[i] = cols[i] - factor * cols[i][j : j + 1, :]
            t = t - factor * t[j : j + 1, :]
        done.append(t[:nb])
        t = t[nb:]
    return jnp.concatenate(done, axis=0)


def factor_solve(a, rhs, nblk=64, nb=16):
    n = a.shape[0]
    rr = lax.broadcasted_iota(jnp.int32, (nblk, nblk), 0)
    cc = lax.broadcasted_iota(jnp.int32, (nblk, nblk), 1)
    eye = jnp.where(rr == cc, 1.0, 0.0).astype(F32)
    full = jnp.concatenate([a, rhs], axis=1)
    parts = []
    for p in range(0, n, nblk):
        t = eliminate(jnp.concatenate([full[:nblk, p : p + nblk], eye], axis=1), nblk, nb)
        d = jnp.sum(jnp.where(rr == cc, t[:, :nblk], 0.0), axis=1, keepdims=True)
        inverse = t[:, nblk:] * lax.rsqrt(d)
        top = mm3(inverse, full[:nblk])
        parts.append(top[:, n:])
        if p + nblk < n:
            lower = mm3(full[nblk:, p : p + nblk], inverse, NT)
            full = full[nblk:] - mm3(lower, top)
    return jnp.concatenate(parts, axis=0)


def kernel(ns, levels, nb_ref, snap, energy, sketch, out, pad, image, modes, joined_image, joined_modes, *scratch):
    (xp, rs_buf, tm_buf, ag_src, ag_buf, gram, halo_sem, rs_sem, tm_sem, ag_sem, im_sem, mo_sem, out_sem, loc_sem) = scratch
    rows = snap.shape[0]
    nblk = rows // K
    piece = K // ns
    scale = 1.0 / (rows * ns)
    t = lax.axis_index("tm")
    s = lax.axis_index("space")
    nt = 2**levels

    def peer(d):
        return lax.rem(s + d, ns)

    def member(level, d):
        size = 2**level
        return (t // size) * size + lax.rem(lax.rem(t, size) + d, size)

    barrier = pltpu.get_barrier_semaphore()

    def greet_space(d, c):
        pl.semaphore_signal(barrier, inc=1, device_id={"space": peer(d)}, device_id_type=pl.DeviceIdType.MESH)
        return c

    def greet_tm(d, c):
        pl.semaphore_signal(barrier, inc=1, device_id={"tm": lax.rem(t + d, nt)}, device_id_type=pl.DeviceIdType.MESH)
        return c

    lax.fori_loop(1, ns, greet_space, 0)
    lax.fori_loop(1, nt, greet_tm, 0)

    def remote(src, dst, send, recv, where):
        return pltpu.make_async_remote_copy(
            src_ref=src, dst_ref=dst, send_sem=send, recv_sem=recv, device_id=where,
            device_id_type=pl.DeviceIdType.MESH,
        )

    halo = HB * K
    pad[halo : halo + rows] = snap[...]
    first = s * nblk

    def image_block(b, source, base):
        last = source.shape[0] // K - 1
        places = [jnp.clip(nb_ref[b, k] - base, 0, last) for k in range(energy.shape[1])]
        blocks = [source[pl.ds(place * K, K), :] for place in places]
        left = jnp.concatenate([energy[b, k] for k in range(energy.shape[1])], axis=1)
        acc = 3.0 * snap[b * K : (b + 1) * K, :].astype(F32) + mm(left, jnp.concatenate(blocks, axis=0))
        image[0][b * K : (b + 1) * K, :] = acc.astype(BF16)

    for b in range(HB, nblk - HB):
        image_block(b, snap, first)

    pl.semaphore_wait(barrier, ns - 1 + nt - 1)

    up = remote(snap.at[0:halo], pad.at[halo + rows :], halo_sem.at[0], halo_sem.at[1], {"space": s - 1})
    down = remote(snap.at[rows - halo :], pad.at[0:halo], halo_sem.at[2], halo_sem.at[3], {"space": s + 1})

    @pl.when(s > 0)
    def _():
        up.start()

    @pl.when(s < ns - 1)
    def _():
        down.start()

    @pl.when(s == 0)
    def _():
        pad[0:halo] = jnp.zeros((halo, K), BF16)

    @pl.when(s == ns - 1)
    def _():
        pad[halo + rows :] = jnp.zeros((halo, K), BF16)

    @pl.when(s > 0)
    def _():
        down.wait_recv()

    @pl.when(s < ns - 1)
    def _():
        up.wait_recv()

    for b in (*range(HB), *range(nblk - HB, nblk)):
        image_block(b, pad, first - HB)

    def whole_sum(level, partial, shadow):
        xp[level] = partial

        def send_piece(d, c):
            q = peer(d)
            remote(
                xp.at[level, pl.ds(q * piece, piece)], rs_buf.at[level, ns - 1 - d],
                rs_sem.at[level, 0], rs_sem.at[level, 1], {"space": q},
            ).start()
            return c

        lax.fori_loop(1, ns, send_piece, 0)
        shadow()
        pltpu.make_async_copy(rs_buf.at[level], rs_buf.at[level], rs_sem.at[level, 1]).wait()
        total = xp[level, pl.ds(s * piece, piece), :]
        for i in range(ns - 1):
            total = total + rs_buf[level, i]
        size = 2**level
        if level:
            ag_src[level, 0] = total

            def send_member(d, c):
                remote(
                    ag_src.at[level, 0], tm_buf[level].at[size - 1 - d],
                    tm_sem.at[level, 0], tm_sem.at[level, 1], {"tm": member(level, d)},
                ).start()
                return c

            lax.fori_loop(1, size, send_member, 0)
            pltpu.make_async_copy(tm_buf[level], tm_buf[level], tm_sem.at[level, 1]).wait()
            for i in range(size - 1):
                total = total + tm_buf[level][i]
        total = total * scale
        ag_src[level, 1] = total

        def send_total(d, c):
            remote(
                ag_src.at[level, 1], ag_buf.at[level, ns - 1 - d],
                ag_sem.at[level, 0], ag_sem.at[level, 1], {"space": peer(d)},
            ).start()
            return c

        lax.fori_loop(1, ns, send_total, 0)
        gram[pl.ds(s * piece, piece), :] = total
        pltpu.make_async_copy(ag_buf.at[level], ag_buf.at[level], ag_sem.at[level, 1]).wait()
        for i in range(ns - 1):
            gram[pl.ds(peer(i + 1) * piece, piece), :] = ag_buf[level, i]
        return gram[...]

    def side_of(level):
        return lax.rem(t // 2 ** (level - 1), 2)

    def exchange(level, source, joined, sem):
        side = side_of(level)
        keep = rows // 2**level
        copy = remote(
            source[level - 1].at[pl.ds((1 - side) * keep, keep)], joined[level - 1].at[side],
            sem.at[level, 0], sem.at[level, 1], {"tm": t + (1 - 2 * side) * 2 ** (level - 1)},
        )
        copy.start()
        joined[level - 1][side] = source[level - 1][pl.ds(side * keep, keep), :]
        return copy

    sends = []
    offset = 0 * t

    def out_own(level, start):
        count = rows // 2**level
        copy = pltpu.make_async_copy(modes[level], out.at[level, 0, pl.ds(start, count)], loc_sem.at[level])
        copy.start()
        sends.append(copy.wait)

    def out_members(level, start):
        count = rows // 2**level
        size = 2**level

        def send_modes(d, c):
            remote(
                modes[level], out.at[level, 0, pl.ds(start, count)],
                out_sem.at[level, 0], out_sem.at[level, 1], {"tm": member(level, d)},
            ).start()
            return c

        lax.fori_loop(1, size, send_modes, 0)
        some = out.at[level, 0, 0 : rows - count]
        sends.append(pltpu.make_async_copy(some, some, out_sem.at[level, 0]).wait)
        sends.append(pltpu.make_async_copy(some, some, out_sem.at[level, 1]).wait)

    rr = lax.broadcasted_iota(jnp.int32, (K, K), 0)
    cc = lax.broadcasted_iota(jnp.int32, (K, K), 1)
    eye = jnp.where(rr == cc, 1.0, 0.0).astype(F32)
    first_gram = whole_sum(0, mm(image[0][...], image[0][...], TN), lambda: None)
    coef = factor_solve(first_gram, eye).astype(BF16)
    image[0][...] = mm(image[0][...], coef, NT).astype(BF16)
    image_copy = exchange(1, image, joined_image, im_sem)
    modes[0][...] = mm(snap[...], coef, NT).astype(BF16)
    modes_copy = exchange(1, modes, joined_modes, mo_sem)
    out_own(0, offset)

    for level in range(1, levels + 1):
        image_copy.wait_recv()
        sends.append(image_copy.wait_send)
        sends.append(modes_copy.wait_send)
        ji = joined_image[level - 1]
        jm = joined_modes[level - 1]
        st = sketch[level - 1]
        before = functools.partial(out_members, level - 1, offset) if level > 1 else (lambda: None)
        x = whole_sum(level, mm(ji[0], ji[1], TN), before)
        st0, st1 = st[:, :K], st[:, K:]
        y0 = st0 + mm3(st1, x, NT)
        y1 = st1 + mm3(st0, x)
        z0 = y0 + mm3(y1, x, NT)
        z1 = y1 + mm3(y0, x)
        y = jnp.concatenate([y0, y1], axis=1)
        z = jnp.concatenate([z0, z1], axis=1)
        coef = factor_solve(mm3(y, z, NT), y).astype(BF16)
        c0, c1 = coef[:, :K], coef[:, K:]
        offset = offset + side_of(level) * (rows // 2**level)
        if level < levels:
            image[level][...] = (mm(ji[0], c0, NT) + mm(ji[1], c1, NT)).astype(BF16)
            image_copy = exchange(level + 1, image, joined_image, im_sem)
        modes_copy.wait_recv()
        modes[level][...] = (mm(jm[0], c0, NT) + mm(jm[1], c1, NT)).astype(BF16)
        if level < levels:
            modes_copy = exchange(level + 1, modes, joined_modes, mo_sem)
        out_own(level, offset)
    out_members(levels, offset)

    @pl.when(s > 0)
    def _():
        up.wait_send()

    @pl.when(s < ns - 1)
    def _():
        down.wait_send()

    for level in range(levels + 1):
        pltpu.make_async_copy(rs_buf.at[level], rs_buf.at[level], rs_sem.at[level, 0]).wait()
        if level:
            pltpu.make_async_copy(tm_buf[level], tm_buf[level], tm_sem.at[level, 0]).wait()
        pltpu.make_async_copy(ag_buf.at[level], ag_buf.at[level], ag_sem.at[level, 0]).wait()
    for wait in sends:
        wait()


def on_device(ns, levels, snapshots, energy, neighbours, sketch):
    rows = snapshots.shape[0]
    count = levels + 1
    piece = K // ns
    chunk = lambda l: pltpu.VMEM((rows // 2**l, K), BF16)
    pair = lambda l: pltpu.VMEM((2, rows // 2**l, K), BF16)
    sems = lambda *shape: pltpu.SemaphoreType.DMA(shape)
    vmem = pl.BlockSpec(memory_space=pltpu.VMEM)
    return pl.pallas_call(
        functools.partial(kernel, ns, levels),
        out_shape=jax.ShapeDtypeStruct((count, 1, rows, K), BF16),
        in_specs=[pl.BlockSpec(memory_space=pltpu.SMEM), vmem, vmem, vmem],
        out_specs=pl.BlockSpec(memory_space=pl.ANY),
        scratch_shapes=[
            pltpu.VMEM((rows + 2 * HB * K, K), BF16),
            [chunk(l) for l in range(count)],
            [chunk(l) for l in range(count)],
            [pair(l) for l in range(1, count)],
            [pair(l) for l in range(1, count)],
            pltpu.VMEM((count, K, K), F32),
            pltpu.VMEM((count, ns - 1, piece, K), F32),
            [pltpu.VMEM((max(2**l - 1, 1), piece, K), F32) for l in range(count)],
            pltpu.VMEM((count, 2, piece, K), F32),
            pltpu.VMEM((count, ns - 1, piece, K), F32),
            pltpu.VMEM((K, K), F32),
            sems(4),
            sems(count, 2),
            sems(count, 2),
            sems(count, 2),
            sems(count, 2),
            sems(count, 2),
            sems(count, 2),
            sems(count),
        ],
        compiler_params=pltpu.CompilerParams(
            collective_id=0, has_side_effects=True, vmem_limit_bytes=40 * 1024 * 1024
        ),
    )(neighbours, snapshots, energy, jnp.swapaxes(sketch, 1, 2))


def solution(mesh):
    placed = (P("space", "tm"), P("space", None, None, None), P("space", None), P())
    ns = mesh.shape["space"]
    levels = mesh.shape["tm"].bit_length() - 1
    return jax.shard_map(
        functools.partial(on_device, ns, levels),
        mesh=mesh,
        in_specs=placed,
        out_specs=P(None, "tm", "space", None),
        check_vma=False,
    )
```

time: 1000 us -> 178 us (0.18)
  waiting for transfers between devices: 735 us -> 0 us
  Pallas kernels: 0 us -> 172 us
  other arithmetic: 141 us -> 0 us
  starting transfers between devices: 59.5 us -> 0 us
  matrix products: 37.6 us -> 0 us
  between operations: 14.6 us -> 0.03 us
    psum x6 -> x0, waiting for transfers between devices: 659 us -> none  [the longest x5 540 us: on_device(): gram_matrix = lax.psum(gram_of(joined_image), 'space') / total_rows]
    pallas_call x0 -> x1, Pallas kernels: none -> 172 us  [on_device(): pl.pallas_call(functools.partial(kernel, ns, levels), out_shape=jax.Shape...]
    another operation x30 -> x0, other arithmetic: 137 us -> none  [the longest x15 62 us: on_device(): lower_factor = jnp.linalg.cholesky(inner_gram)]
    ppermute x12 -> x0, waiting for transfers between devices: 75.5 us -> none  [the longest x10 75.4 us: from_partner(): return lax.ppermute(value, axis, pairs)]
    ppermute x12 -> x0, starting transfers between devices: 58.9 us -> none  [the longest x10 52.9 us: from_partner(): return lax.ppermute(value, axis, pairs)]
    dot_general x39 -> x0, matrix products: 35.8 us -> none  [the longest x6 7.81 us: gram_of(): jnp.einsum('rc,rd->cd', energy_image, energy_image, preferred_element_typ...]
  transfers between devices with their start and end apart: 18 -> 0, of which waited for: 13 -> 0; matrix products, arithmetic and copies ran while one was open for 9% -> 0% of each run, Pallas kernels for 0% -> 0%
where the time goes in v1:
time: 178 us
  Pallas kernels  172 us (97%)
  local copies, waits for them, and re-layouts  5.59 us (3%)
    pallas_call x1, Pallas kernels, on_device(): pl.pallas_call(functools.partial(kernel, ns, levels), out_shape=jax.Shape...  172 us
    unnamed x8, local copies, waits for them, and re-layouts  5.59 us

profile of v1, /device:TPU:1, one launch (start us, length us, event | category | flops | bytes accessed | tf_op | source)
XLA Modules:
  0.0 177.7 jit_solution(11160701760343455033)
XLA Ops:
  0.0 1.3 copy.5
  1.3 0.0 copy-start
  1.3 1.5 copy-done
  2.8 0.0 copy-start.1
  2.8 0.9 copy-done.1
  3.8 0.0 copy-start.2
  3.8 0.7 copy-done.2
  4.5 172.1 %shard_map.46 = bf16[6,1,1024,128]{3,2,1,0:T(8,128)(2,1)S(1)} custom-call(s32[8,7]{1,0:T(8,128)S(1)} %copy-done.2, bf16[1024,128]{1,0:T(8,128)(2,1)S(1)} %copy-done.1, bf16[8,7,128,128]{3,2,1,0:T(8,128)(2,1)S(1)} %copy-done, f32[5,128,256]{2,1,0:T(8,128)S(1)} %bitcast.1), custom_call_target="tpu_custom_call" | custom-call | tf_op jit(solution)/shard_map/pallas_call | solution.py:305
  176.6 1.1 copy.7
Async XLA Ops:
  1.3 1.5 copy-start
  2.8 0.9 copy-start.1
  3.8 0.7 copy-start.2

commit v2 on v1

--- a/solution.py
+++ b/solution.py
@@ -66,15 +66,25 @@
     return jnp.concatenate(parts, axis=0)
 
 
-def kernel(ns, levels, nb_ref, snap, energy, sketch, out, pad, image, modes, joined_image, joined_modes, *scratch):
-    (xp, rs_buf, tm_buf, ag_src, ag_buf, gram, halo_sem, rs_sem, tm_sem, ag_sem, im_sem, mo_sem, out_sem, loc_sem) = scratch
+def kernel(ns, levels, nb_ref, snap_hbm, energy_hbm, sketch_hbm, out, snap, energy, sketch, sketch_t, pad, *scratch):
+    (image, gathered, last_modes, joined_image, joined_modes, xp, rs_buf, tm_buf, ag_src, ag_buf, gram) = scratch[:11]
+    (in_sem, halo_sem, rs_sem, tm_sem, ag_sem, im_sem, mo_sem, ga_sem, sib_sem, out_sem) = scratch[11:]
     rows = snap.shape[0]
+    half = rows // 2
     nblk = rows // K
     piece = K // ns
     scale = 1.0 / (rows * ns)
     t = lax.axis_index("tm")
     s = lax.axis_index("space")
     nt = 2**levels
+    core = lax.rem(t, 2)
+    halo = HB * K
+    pads = pltpu.make_async_copy(snap_hbm, pad.at[pl.ds(halo, rows)], in_sem.at[0])
+    loads = [
+        pltpu.make_async_copy(snap_hbm, snap, in_sem.at[1]),
+        pltpu.make_async_copy(energy_hbm, energy, in_sem.at[2]),
+        pltpu.make_async_copy(sketch_hbm, sketch, in_sem.at[3]),
+    ]
 
     def peer(d):
         return lax.rem(s + d, ns)
@@ -93,8 +103,11 @@
         pl.semaphore_signal(barrier, inc=1, device_id={"tm": lax.rem(t + d, nt)}, device_id_type=pl.DeviceIdType.MESH)
         return c
 
+    lax.fori_loop(1, nt, greet_tm, 0)
     lax.fori_loop(1, ns, greet_space, 0)
-    lax.fori_loop(1, nt, greet_tm, 0)
+    for load in loads:
+        load.start()
+    pads.start()
 
     def remote(src, dst, send, recv, where):
         return pltpu.make_async_remote_copy(
@@ -102,8 +115,6 @@
             device_id_type=pl.DeviceIdType.MESH,
         )
 
-    halo = HB * K
-    pad[halo : halo + rows] = snap[...]
     first = s * nblk
 
     def image_block(b, source, base):
@@ -114,8 +125,13 @@
         acc = 3.0 * snap[b * K : (b + 1) * K, :].astype(F32) + mm(left, jnp.concatenate(blocks, axis=0))
         image[0][b * K : (b + 1) * K, :] = acc.astype(BF16)
 
+    for load in loads:
+        load.wait()
     for b in range(HB, nblk - HB):
         image_block(b, snap, first)
+    for l in range(levels):
+        sketch_t[l] = sketch[l].T
+    pads.wait()
 
     pl.semaphore_wait(barrier, ns - 1 + nt - 1)
 
@@ -201,41 +217,61 @@
     def side_of(level):
         return lax.rem(t // 2 ** (level - 1), 2)
 
-    def exchange(level, source, joined, sem):
+    sends = []
+
+    def exchange(level, source, start, joined, sem):
         side = side_of(level)
         keep = rows // 2**level
         copy = remote(
-            source[level - 1].at[pl.ds((1 - side) * keep, keep)], joined[level - 1].at[side],
+            source.at[pl.ds(start + (1 - side) * keep, keep)], joined.at[side],
             sem.at[level, 0], sem.at[level, 1], {"tm": t + (1 - 2 * side) * 2 ** (level - 1)},
         )
         copy.start()
-        joined[level - 1][side] = source[level - 1][pl.ds(side * keep, keep), :]
+        joined[side] = source[pl.ds(start + side * keep, keep), :]
+        sends.append(copy.wait_send)
         return copy
 
-    sends = []
-    offset = 0 * t
-
-    def out_own(level, start):
+    def slot_of(level):
+        return side_of(levels) if level == levels - 1 else 0
+
+    def gather(level, start):
         count = rows // 2**level
-        copy = pltpu.make_async_copy(modes[level], out.at[level, 0, pl.ds(start, count)], loc_sem.at[level])
+        both = level == levels - 1
+        size = 2 ** (level + 1) if both else 2**level
+        mine = gathered[level].at[slot_of(level), pl.ds(start, count)]
+
+        def send_modes(d, c):
+            remote(
+                mine, mine, ga_sem.at[level, 0], ga_sem.at[level, 1],
+                {"tm": (t // size) * size + lax.rem(lax.rem(t, size) + 2 * d, size)},
+            ).start()
+            return c
+
+        lax.fori_loop(1, size // 2, send_modes, 0)
+
+    def gather_bytes(level, i):
+        count = rows // 2**level
+        size = 2 ** (level + 1) if level == levels - 1 else 2**level
+        some = gathered[level].at[0, 0 : (size // 2 - 1) * count]
+        return pltpu.make_async_copy(some, some, ga_sem.at[level, i])
+
+    def needs_gather(level):
+        return level > 1 or level == levels - 1
+
+    def to_sibling(level):
+        if needs_gather(level):
+            gather_bytes(level, 1).wait()
+            sends.append(gather_bytes(level, 0).wait)
+        mine = gathered[level].at[:, pl.ds(core * half, half)]
+        copy = remote(mine, mine, sib_sem.at[level, 0], sib_sem.at[level, 1], {"tm": t + 1 - 2 * core})
+        copy.start()
+        sends.append(copy.wait_send)
+        return copy
+
+    def store(level):
+        copy = pltpu.make_async_copy(gathered[level].at[slot_of(level)], out.at[level, 0], out_sem.at[level])
         copy.start()
         sends.append(copy.wait)
-
-    def out_members(level, start):
-        count = rows // 2**level
-        size = 2**level
-
-        def send_modes(d, c):
-            remote(
-                modes[level], out.at[level, 0, pl.ds(start, count)],
-                out_sem.at[level, 0], out_sem.at[level, 1], {"tm": member(level, d)},
-            ).start()
-            return c
-
-        lax.fori_loop(1, size, send_modes, 0)
-        some = out.at[level, 0, 0 : rows - count]
-        sends.append(pltpu.make_async_copy(some, some, out_sem.at[level, 0]).wait)
-        sends.append(pltpu.make_async_copy(some, some, out_sem.at[level, 1]).wait)
 
     rr = lax.broadcasted_iota(jnp.int32, (K, K), 0)
     cc = lax.broadcasted_iota(jnp.int32, (K, K), 1)
@@ -243,20 +279,29 @@
     first_gram = whole_sum(0, mm(image[0][...], image[0][...], TN), lambda: None)
     coef = factor_solve(first_gram, eye).astype(BF16)
     image[0][...] = mm(image[0][...], coef, NT).astype(BF16)
-    image_copy = exchange(1, image, joined_image, im_sem)
-    modes[0][...] = mm(snap[...], coef, NT).astype(BF16)
-    modes_copy = exchange(1, modes, joined_modes, mo_sem)
-    out_own(0, offset)
-
+    image_copy = exchange(1, image[0], 0, joined_image[0], im_sem)
+    gathered[0][0] = mm(snap[...], coef, NT).astype(BF16)
+    modes_copy = exchange(1, gathered[0].at[0], 0, joined_modes[0], mo_sem)
+    store(0)
+
+    offset = 0 * t
+    siblings = {}
     for level in range(1, levels + 1):
         image_copy.wait_recv()
-        sends.append(image_copy.wait_send)
-        sends.append(modes_copy.wait_send)
         ji = joined_image[level - 1]
         jm = joined_modes[level - 1]
-        st = sketch[level - 1]
-        before = functools.partial(out_members, level - 1, offset) if level > 1 else (lambda: None)
-        x = whole_sum(level, mm(ji[0], ji[1], TN), before)
+
+        def shadow(level=level, start=offset):
+            if level - 1 >= 1 and needs_gather(level - 1):
+                gather(level - 1, start)
+            if level - 2 >= 1:
+                siblings[level - 2].wait_recv()
+                store(level - 2)
+
+        x = whole_sum(level, mm(ji[0], ji[1], TN), shadow)
+        if level - 1 >= 1:
+            siblings[level - 1] = to_sibling(level - 1)
+        st = sketch_t[level - 1]
         st0, st1 = st[:, :K], st[:, K:]
         y0 = st0 + mm3(st1, x, NT)
         y1 = st1 + mm3(st0, x)
@@ -266,16 +311,26 @@
         z = jnp.concatenate([z0, z1], axis=1)
         coef = factor_solve(mm3(y, z, NT), y).astype(BF16)
         c0, c1 = coef[:, :K], coef[:, K:]
-        offset = offset + side_of(level) * (rows // 2**level)
+        keep = rows // 2**level
+        offset = offset + side_of(level) * keep
         if level < levels:
             image[level][...] = (mm(ji[0], c0, NT) + mm(ji[1], c1, NT)).astype(BF16)
-            image_copy = exchange(level + 1, image, joined_image, im_sem)
-        modes_copy.wait_recv()
-        modes[level][...] = (mm(jm[0], c0, NT) + mm(jm[1], c1, NT)).astype(BF16)
-        if level < levels:
-            modes_copy = exchange(level + 1, modes, joined_modes, mo_sem)
-        out_own(level, offset)
-    out_members(levels, offset)
+            image_copy = exchange(level + 1, image[level], 0, joined_image[level], im_sem)
+            modes_copy.wait_recv()
+            target = gathered[level].at[slot_of(level)]
+            target[pl.ds(offset, keep), :] = (mm(jm[0], c0, NT) + mm(jm[1], c1, NT)).astype(BF16)
+            if level < levels - 1:
+                modes_copy = exchange(level + 1, target, offset, joined_modes[level], mo_sem)
+        else:
+            siblings[level - 1].wait_recv()
+            store(level - 1)
+            pair = gathered[level - 1]
+            for i in range(4):
+                part = slice(i * rows // 4, (i + 1) * rows // 4)
+                last_modes[part] = (mm(pair[0, part], c0, NT) + mm(pair[1, part], c1, NT)).astype(BF16)
+                copy = pltpu.make_async_copy(last_modes.at[part], out.at[level, 0, part], out_sem.at[level + i])
+                copy.start()
+                sends.append(copy.wait)
 
     @pl.when(s > 0)
     def _():
@@ -298,21 +353,24 @@
     rows = snapshots.shape[0]
     count = levels + 1
     piece = K // ns
-    chunk = lambda l: pltpu.VMEM((rows // 2**l, K), BF16)
-    pair = lambda l: pltpu.VMEM((2, rows // 2**l, K), BF16)
     sems = lambda *shape: pltpu.SemaphoreType.DMA(shape)
-    vmem = pl.BlockSpec(memory_space=pltpu.VMEM)
+    hbm = pl.BlockSpec(memory_space=pltpu.HBM)
     return pl.pallas_call(
         functools.partial(kernel, ns, levels),
         out_shape=jax.ShapeDtypeStruct((count, 1, rows, K), BF16),
-        in_specs=[pl.BlockSpec(memory_space=pltpu.SMEM), vmem, vmem, vmem],
-        out_specs=pl.BlockSpec(memory_space=pl.ANY),
+        in_specs=[pl.BlockSpec(memory_space=pltpu.SMEM), hbm, hbm, hbm],
+        out_specs=hbm,
         scratch_shapes=[
+            pltpu.VMEM(snapshots.shape, BF16),
+            pltpu.VMEM(energy.shape, BF16),
+            pltpu.VMEM(sketch.shape, F32),
+            pltpu.VMEM((levels, K, 2 * K), F32),
             pltpu.VMEM((rows + 2 * HB * K, K), BF16),
-            [chunk(l) for l in range(count)],
-            [chunk(l) for l in range(count)],
-            [pair(l) for l in range(1, count)],
-            [pair(l) for l in range(1, count)],
+            [pltpu.VMEM((rows // 2**l, K), BF16) for l in range(levels)],
+            [pltpu.VMEM((2 if l == levels - 1 else 1, rows, K), BF16) for l in range(levels)],
+            pltpu.VMEM((rows, K), BF16),
+            [pltpu.VMEM((2, rows // 2**l, K), BF16) for l in range(1, count)],
+            [pltpu.VMEM((2, rows // 2**l, K), BF16) for l in range(1, count)],
             pltpu.VMEM((count, K, K), F32),
             pltpu.VMEM((count, ns - 1, piece, K), F32),
             [pltpu.VMEM((max(2**l - 1, 1), piece, K), F32) for l in range(count)],
@@ -320,18 +378,14 @@
             pltpu.VMEM((count, ns - 1, piece, K), F32),
             pltpu.VMEM((K, K), F32),
             sems(4),
-            sems(count, 2),
-            sems(count, 2),
-            sems(count, 2),
-            sems(count, 2),
-            sems(count, 2),
-            sems(count, 2),
-            sems(count),
+            sems(4),
+            *[sems(count, 2)] * 7,
+            sems(count + 4),
         ],
         compiler_params=pltpu.CompilerParams(
             collective_id=0, has_side_effects=True, vmem_limit_bytes=40 * 1024 * 1024
         ),
-    )(neighbours, snapshots, energy, jnp.swapaxes(sketch, 1, 2))
+    )(neighbours, snapshots, energy, sketch)
 
 
 def solution(mesh):

time: 178 us -> 166 us (0.933)
  Pallas kernels: 172 us -> 161 us
    pallas_call x1, Pallas kernels: 172 us -> 161 us  [on_device(): pl.pallas_call(functools.partial(kernel, ns, levels), out_shape=jax.Shape...]
    unnamed x8 -> x9, local copies, waits for them, and re-layouts: 5.59 us -> 5.37 us
where the time goes in v2:
time: 166 us
  Pallas kernels  161 us (97%)
  local copies, waits for them, and re-layouts  5.37 us (3%)
    pallas_call x1, Pallas kernels, on_device(): pl.pallas_call(functools.partial(kernel, ns, levels), out_shape=jax.Shape...  161 us
    unnamed x9, local copies, waits for them, and re-layouts  5.37 us

profile of v2, /device:TPU:1, one launch (start us, length us, event | category | flops | bytes accessed | tf_op | source)
XLA Modules:
  0.0 166.2 jit_solution(9018234841550992734)
XLA Ops:
  0.0 0.0 copy-start
  0.0 1.5 copy-done
  1.5 0.0 copy-start.1
  1.5 1.1 copy-done.1
  2.6 0.0 copy-start.2
  2.6 0.9 copy-done.2
  3.5 0.0 copy-start.3
  3.5 0.7 copy-done.3
  4.2 160.8 %shard_map.46 = bf16[6,1,1024,128]{3,2,1,0:T(8,128)(2,1)S(1)} custom-call(s32[8,7]{1,0:T(8,128)S(1)} %copy-done.3, bf16[1024,128]{1,0:T(8,128)(2,1)S(1)} %copy-done.2, bf16[8,7,128,128]{3,2,1,0:T(8,128)(2,1)S(1)} %copy-done, f32[5,256,128]{2,1,0:T(8,128)S(1)} %copy-done.1), custom_call_target="tpu_custom_call" | custom-call | tf_op jit(solution)/shard_map/pallas_call | solution.py:358
  165.1 1.1 copy.6
Async XLA Ops:
  0.0 1.5 copy-start
  1.5 1.1 copy-start.1
  2.6 0.9 copy-start.2
  3.5 0.7 copy-start.3

commit v3 on v2

--- a/solution.py
+++ b/solution.py
@@ -9,6 +9,7 @@
 
 K = 128
 HB = 2
+CAP = 3
 F32 = jnp.float32
 BF16 = jnp.bfloat16
 NN = ((1,), (0,))
@@ -29,6 +30,11 @@
     ah, al = split(a)
     bh, bl = split(b)
     return mm(ah, bh, dims) + (mm(ah, bl, dims) + mm(al, bh, dims))
+
+
+def mm2(a, b, dims=NN):
+    ah, al = split(a)
+    return mm(ah, b, dims) + mm(al, b, dims)
 
 
 def eliminate(t, n, nb):
@@ -66,9 +72,14 @@
     return jnp.concatenate(parts, axis=0)
 
 
+def split_of(level):
+    return min(level, CAP)
+
+
 def kernel(ns, levels, nb_ref, snap_hbm, energy_hbm, sketch_hbm, out, snap, energy, sketch, sketch_t, pad, *scratch):
-    (image, gathered, last_modes, joined_image, joined_modes, xp, rs_buf, tm_buf, ag_src, ag_buf, gram) = scratch[:11]
-    (in_sem, halo_sem, rs_sem, tm_sem, ag_sem, im_sem, mo_sem, ga_sem, sib_sem, out_sem) = scratch[11:]
+    (image, gathered, last_modes, joined_energy, joined_image, joined_modes, xp, rs_buf, tm_buf) = scratch[:9]
+    (ag_src, ag_buf, gram, coefs) = scratch[9:13]
+    (in_sem, halo_sem, rs_sem, tm_sem, ag_sem, im_sem, mo_sem, ga_sem, sib_sem, co_sem, out_sem) = scratch[13:]
     rows = snap.shape[0]
     half = rows // 2
     nblk = rows // K
@@ -165,7 +176,7 @@
     for b in (*range(HB), *range(nblk - HB, nblk)):
         image_block(b, pad, first - HB)
 
-    def whole_sum(level, partial, shadow):
+    def sum_start(level, partial):
         xp[level] = partial
 
         def send_piece(d, c):
@@ -177,23 +188,28 @@
             return c
 
         lax.fori_loop(1, ns, send_piece, 0)
-        shadow()
+
+    def sum_members(level):
         pltpu.make_async_copy(rs_buf.at[level], rs_buf.at[level], rs_sem.at[level, 1]).wait()
         total = xp[level, pl.ds(s * piece, piece), :]
         for i in range(ns - 1):
             total = total + rs_buf[level, i]
-        size = 2**level
+        size = 2 ** split_of(level)
+        ag_src[level, 0] = total
+
+        def send_member(d, c):
+            remote(
+                ag_src.at[level, 0], tm_buf[level].at[size - 1 - d],
+                tm_sem.at[level, 0], tm_sem.at[level, 1], {"tm": member(split_of(level), d)},
+            ).start()
+            return c
+
+        lax.fori_loop(1, size, send_member, 0)
+
+    def sum_back(level):
+        size = 2 ** split_of(level)
+        total = ag_src[level, 0]
         if level:
-            ag_src[level, 0] = total
-
-            def send_member(d, c):
-                remote(
-                    ag_src.at[level, 0], tm_buf[level].at[size - 1 - d],
-                    tm_sem.at[level, 0], tm_sem.at[level, 1], {"tm": member(level, d)},
-                ).start()
-                return c
-
-            lax.fori_loop(1, size, send_member, 0)
             pltpu.make_async_copy(tm_buf[level], tm_buf[level], tm_sem.at[level, 1]).wait()
             for i in range(size - 1):
                 total = total + tm_buf[level][i]
@@ -208,7 +224,9 @@
             return c
 
         lax.fori_loop(1, ns, send_total, 0)
-        gram[pl.ds(s * piece, piece), :] = total
+
+    def sum_end(level):
+        gram[pl.ds(s * piece, piece), :] = ag_src[level, 1]
         pltpu.make_async_copy(ag_buf.at[level], ag_buf.at[level], ag_sem.at[level, 1]).wait()
         for i in range(ns - 1):
             gram[pl.ds(peer(i + 1) * piece, piece), :] = ag_buf[level, i]
@@ -221,49 +239,46 @@
 
     def exchange(level, source, start, joined, sem):
         side = side_of(level)
-        keep = rows // 2**level
+        keep = rows // 2 ** split_of(level)
+        other, own = ((1 - side) * keep, side * keep) if level <= CAP else (0, 0)
         copy = remote(
-            source.at[pl.ds(start + (1 - side) * keep, keep)], joined.at[side],
+            source.at[pl.ds(start + other, keep)], joined.at[side],
             sem.at[level, 0], sem.at[level, 1], {"tm": t + (1 - 2 * side) * 2 ** (level - 1)},
         )
         copy.start()
-        joined[side] = source[pl.ds(start + side * keep, keep), :]
+        joined[side] = source[pl.ds(start + own, keep), :]
         sends.append(copy.wait_send)
         return copy
 
     def slot_of(level):
         return side_of(levels) if level == levels - 1 else 0
 
+    def mine(level, start):
+        return gathered[level].at[:, pl.ds(start, rows // 2 ** split_of(level))]
+
     def gather(level, start):
-        count = rows // 2**level
-        both = level == levels - 1
-        size = 2 ** (level + 1) if both else 2**level
-        mine = gathered[level].at[slot_of(level), pl.ds(start, count)]
+        size = 2 ** split_of(level)
 
         def send_modes(d, c):
             remote(
-                mine, mine, ga_sem.at[level, 0], ga_sem.at[level, 1],
-                {"tm": (t // size) * size + lax.rem(lax.rem(t, size) + 2 * d, size)},
+                mine(level, start), mine(level, start), ga_sem.at[level, 0], ga_sem.at[level, 1],
+                {"tm": member(split_of(level), 2 * d)},
             ).start()
             return c
 
         lax.fori_loop(1, size // 2, send_modes, 0)
 
     def gather_bytes(level, i):
-        count = rows // 2**level
-        size = 2 ** (level + 1) if level == levels - 1 else 2**level
-        some = gathered[level].at[0, 0 : (size // 2 - 1) * count]
+        count = rows // 2 ** split_of(level)
+        some = gathered[level].at[:, 0 : (2 ** split_of(level) // 2 - 1) * count]
         return pltpu.make_async_copy(some, some, ga_sem.at[level, i])
 
-    def needs_gather(level):
-        return level > 1 or level == levels - 1
-
     def to_sibling(level):
-        if needs_gather(level):
+        if split_of(level) > 1:
             gather_bytes(level, 1).wait()
             sends.append(gather_bytes(level, 0).wait)
-        mine = gathered[level].at[:, pl.ds(core * half, half)]
-        copy = remote(mine, mine, sib_sem.at[level, 0], sib_sem.at[level, 1], {"tm": t + 1 - 2 * core})
+        whole = gathered[level].at[:, pl.ds(core * half, half)]
+        copy = remote(whole, whole, sib_sem.at[level, 0], sib_sem.at[level, 1], {"tm": t + 1 - 2 * core})
         copy.start()
         sends.append(copy.wait_send)
         return copy
@@ -276,10 +291,19 @@
     rr = lax.broadcasted_iota(jnp.int32, (K, K), 0)
     cc = lax.broadcasted_iota(jnp.int32, (K, K), 1)
     eye = jnp.where(rr == cc, 1.0, 0.0).astype(F32)
-    first_gram = whole_sum(0, mm(image[0][...], image[0][...], TN), lambda: None)
-    coef = factor_solve(first_gram, eye).astype(BF16)
-    image[0][...] = mm(image[0][...], coef, NT).astype(BF16)
-    image_copy = exchange(1, image[0], 0, joined_image[0], im_sem)
+    energy_copy = exchange(1, image[0], 0, joined_energy, im_sem)
+    sum_start(0, mm(image[0][...], image[0][...], TN))
+    energy_copy.wait_recv()
+    sum_start(1, mm(joined_energy[0], joined_energy[1], TN))
+    sum_members(0)
+    sum_back(0)
+    sum_members(1)
+    sum_back(1)
+    coef = factor_solve(sum_end(0), eye).astype(BF16)
+    coefs[core] = coef
+    coefs_copy = remote(coefs.at[core], coefs.at[core], co_sem.at[0], co_sem.at[1], {"tm": t + 1 - 2 * core})
+    coefs_copy.start()
+    sends.append(coefs_copy.wait_send)
     gathered[0][0] = mm(snap[...], coef, NT).astype(BF16)
     modes_copy = exchange(1, gathered[0].at[0], 0, joined_modes[0], mo_sem)
     store(0)
@@ -287,19 +311,28 @@
     offset = 0 * t
     siblings = {}
     for level in range(1, levels + 1):
-        image_copy.wait_recv()
         ji = joined_image[level - 1]
         jm = joined_modes[level - 1]
-
-        def shadow(level=level, start=offset):
-            if level - 1 >= 1 and needs_gather(level - 1):
-                gather(level - 1, start)
+        if level == 1:
+            coefs_copy.wait_recv()
+            for i in range(2):
+                ji[i] = mm(joined_energy[i], coefs[i], NT).astype(BF16)
+            x = mm2(mm2(sum_end(1), coefs[1], NT).T, coefs[0], NT).T
+        else:
+            image_copy.wait_recv()
+            sum_start(level, mm(ji[0], ji[1], TN))
+            if level - 1 >= 1 and level < levels and split_of(level - 1) > 1:
+                gather(level - 1, offset)
             if level - 2 >= 1:
                 siblings[level - 2].wait_recv()
                 store(level - 2)
-
-        x = whole_sum(level, mm(ji[0], ji[1], TN), shadow)
-        if level - 1 >= 1:
+            sum_members(level)
+            if level == levels:
+                modes_copy.wait_recv()
+                if split_of(level - 1) > 1:
+                    gather(level - 1, offset)
+            sum_back(level)
+            x = sum_end(level)
             siblings[level - 1] = to_sibling(level - 1)
         st = sketch_t[level - 1]
         st0, st1 = st[:, :K], st[:, K:]
@@ -311,8 +344,9 @@
         z = jnp.concatenate([z0, z1], axis=1)
         coef = factor_solve(mm3(y, z, NT), y).astype(BF16)
         c0, c1 = coef[:, :K], coef[:, K:]
-        keep = rows // 2**level
-        offset = offset + side_of(level) * keep
+        keep = rows // 2 ** split_of(level)
+        if level <= CAP:
+            offset = offset + side_of(level) * keep
         if level < levels:
             image[level][...] = (mm(ji[0], c0, NT) + mm(ji[1], c1, NT)).astype(BF16)
             image_copy = exchange(level + 1, image[level], 0, joined_image[level], im_sem)
@@ -321,6 +355,15 @@
             target[pl.ds(offset, keep), :] = (mm(jm[0], c0, NT) + mm(jm[1], c1, NT)).astype(BF16)
             if level < levels - 1:
                 modes_copy = exchange(level + 1, target, offset, joined_modes[level], mo_sem)
+            else:
+                side = side_of(levels)
+                chunk = target.at[pl.ds(offset, keep)]
+                modes_copy = remote(
+                    chunk, chunk, mo_sem.at[levels, 0], mo_sem.at[levels, 1],
+                    {"tm": t + (1 - 2 * side) * 2 ** (levels - 1)},
+                )
+                modes_copy.start()
+                sends.append(modes_copy.wait_send)
         else:
             siblings[level - 1].wait_recv()
             store(level - 1)
@@ -351,6 +394,7 @@
 
 def on_device(ns, levels, snapshots, energy, neighbours, sketch):
     rows = snapshots.shape[0]
+    half = rows // 2
     count = levels + 1
     piece = K // ns
     sems = lambda *shape: pltpu.SemaphoreType.DMA(shape)
@@ -366,20 +410,23 @@
             pltpu.VMEM(sketch.shape, F32),
             pltpu.VMEM((levels, K, 2 * K), F32),
             pltpu.VMEM((rows + 2 * HB * K, K), BF16),
-            [pltpu.VMEM((rows // 2**l, K), BF16) for l in range(levels)],
+            [pltpu.VMEM((rows // 2 ** split_of(l), K), BF16) for l in range(levels)],
             [pltpu.VMEM((2 if l == levels - 1 else 1, rows, K), BF16) for l in range(levels)],
             pltpu.VMEM((rows, K), BF16),
-            [pltpu.VMEM((2, rows // 2**l, K), BF16) for l in range(1, count)],
-            [pltpu.VMEM((2, rows // 2**l, K), BF16) for l in range(1, count)],
+            pltpu.VMEM((2, half, K), BF16),
+            [pltpu.VMEM((2, rows // 2 ** split_of(l), K), BF16) for l in range(1, count)],
+            [pltpu.VMEM((2, rows // 2 ** split_of(l), K), BF16) for l in range(1, count)],
             pltpu.VMEM((count, K, K), F32),
             pltpu.VMEM((count, ns - 1, piece, K), F32),
-            [pltpu.VMEM((max(2**l - 1, 1), piece, K), F32) for l in range(count)],
+            [pltpu.VMEM((max(2 ** split_of(l) - 1, 1), piece, K), F32) for l in range(count)],
             pltpu.VMEM((count, 2, piece, K), F32),
             pltpu.VMEM((count, ns - 1, piece, K), F32),
             pltpu.VMEM((K, K), F32),
+            pltpu.VMEM((2, K, K), BF16),
             sems(4),
             sems(4),
             *[sems(count, 2)] * 7,
+            sems(2),
             sems(count + 4),
         ],
         compiler_params=pltpu.CompilerParams(

time: 166 us -> 145 us (0.87)
  Pallas kernels: 161 us -> 139 us
    pallas_call x1, Pallas kernels: 161 us -> 139 us  [on_device(): pl.pallas_call(functools.partial(kernel, ns, levels), out_shape=jax.Shape...]
where the time goes in v3:
time: 145 us; the launch traced here: 144 us
  Pallas kernels  139 us (96%)
  local copies, waits for them, and re-layouts  5.37 us (4%)
    pallas_call x1, Pallas kernels, on_device(): pl.pallas_call(functools.partial(kernel, ns, levels), out_shape=jax.Shape...  139 us
    unnamed x9, local copies, waits for them, and re-layouts  5.37 us

profile of v3, /device:TPU:1, one launch (start us, length us, event | category | flops | bytes accessed | tf_op | source)
XLA Modules:
  0.0 144.5 jit_solution(18086693960668188675)
XLA Ops:
  0.0 0.0 copy-start
  0.0 1.5 %copy-done = bf16[8,7,128,128]{3,2,1,0:T(8,128)(2,1)S(1)} copy-done((bf16[8,7,128,128]{3,2,1,0:T(8,128)(2,1)S(1)}, bf16[8,7,128,128]{3,2,1,0:T(8,128)(2,1)}, u32[]{:S(2)}) %copy-start) | copy-done | bytes 1835032
  1.5 0.0 copy-start.1
  1.5 1.1 copy-done.1
  2.6 0.0 copy-start.2
  2.6 0.9 copy-done.2
  3.5 0.0 copy-start.3
  3.5 0.7 copy-done.3
  4.2 139.1 %shard_map.46 = bf16[6,1,1024,128]{3,2,1,0:T(8,128)(2,1)S(1)} custom-call(s32[8,7]{1,0:T(8,128)S(1)} %copy-done.3, bf16[1024,128]{1,0:T(8,128)(2,1)S(1)} %copy-done.2, bf16[8,7,128,128]{3,2,1,0:T(8,128)(2,1)S(1)} %copy-done, f32[5,256,128]{2,1,0:T(8,128)S(1)} %copy-done.1), custom_call_target="tpu_custom_call" | custom-call | tf_op jit(solution)/shard_map/pallas_call | solution.py:402
  143.3 1.1 copy.6
Async XLA Ops:
  0.0 1.5 %copy-start = (bf16[8,7,128,128]{3,2,1,0:T(8,128)(2,1)S(1)}, bf16[8,7,128,128]{3,2,1,0:T(8,128)(2,1)}, u32[]{:S(2)}) copy-start(bf16[8,7,128,128]{3,2,1,0:T(8,128)(2,1)} %energy_hbm.1) | copy-start | bytes 5505028
  1.5 1.1 copy-start.1
  2.6 0.9 copy-start.2
  3.5 0.7 copy-start.3

commit v4 on v3

--- a/solution.py
+++ b/solution.py
@@ -10,6 +10,7 @@
 K = 128
 HB = 2
 CAP = 3
+AHEAD = 3
 F32 = jnp.float32
 BF16 = jnp.bfloat16
 NN = ((1,), (0,))
@@ -35,6 +36,11 @@
 def mm2(a, b, dims=NN):
     ah, al = split(a)
     return mm(ah, b, dims) + mm(al, b, dims)
+
+
+def around(a, middle, b):
+    high, low = split(mm2(middle, b, NT))
+    return mm(a, high) + mm(a, low)
 
 
 def eliminate(t, n, nb):
@@ -78,8 +84,9 @@
 
 def kernel(ns, levels, nb_ref, snap_hbm, energy_hbm, sketch_hbm, out, snap, energy, sketch, sketch_t, pad, *scratch):
     (image, gathered, last_modes, joined_energy, joined_image, joined_modes, xp, rs_buf, tm_buf) = scratch[:9]
-    (ag_src, ag_buf, gram, coefs) = scratch[9:13]
-    (in_sem, halo_sem, rs_sem, tm_sem, ag_sem, im_sem, mo_sem, ga_sem, sib_sem, co_sem, out_sem) = scratch[13:]
+    (ag_src, ag_buf, gram, coefs, ahead_rows, ahead_coefs, wide_xp, wide_rs, wide_tm, wide_src) = scratch[9:19]
+    (wide_ag, wide_gram, in_sem, halo_sem, rs_sem, tm_sem, ag_sem, im_sem, mo_sem, ga_sem) = scratch[19:29]
+    (sib_sem, co_sem, ahead_sem, out_sem) = scratch[29:]
     rows = snap.shape[0]
     half = rows // 2
     nblk = rows // K
@@ -97,6 +104,14 @@
         pltpu.make_async_copy(sketch_hbm, sketch, in_sem.at[3]),
     ]
 
+    ny = min(4, ns)
+    nx = ns // ny
+    px, py = s // ny, lax.rem(s, ny)
+    steps = [(dx, dy) for dx in range(nx) for dy in range(ny) if dx or dy]
+    steps.sort(key=lambda step: -min(step[0], nx - step[0]) - min(step[1], ny - step[1]))
+    peers = [lax.rem(px + dx, nx) * ny + lax.rem(py + dy, ny) for dx, dy in steps]
+    senders = [lax.rem(px + nx - dx, nx) * ny + lax.rem(py + ny - dy, ny) for dx, dy in steps]
+
     def peer(d):
         return lax.rem(s + d, ns)
 
@@ -179,15 +194,11 @@
     def sum_start(level, partial):
         xp[level] = partial
 
-        def send_piece(d, c):
-            q = peer(d)
+        for i, q in enumerate(peers):
             remote(
-                xp.at[level, pl.ds(q * piece, piece)], rs_buf.at[level, ns - 1 - d],
+                xp.at[level, pl.ds(q * piece, piece)], rs_buf.at[level, i],
                 rs_sem.at[level, 0], rs_sem.at[level, 1], {"space": q},
             ).start()
-            return c
-
-        lax.fori_loop(1, ns, send_piece, 0)
 
     def sum_members(level):
         pltpu.make_async_copy(rs_buf.at[level], rs_buf.at[level], rs_sem.at[level, 1]).wait()
@@ -216,24 +227,86 @@
         total = total * scale
         ag_src[level, 1] = total
 
-        def send_total(d, c):
+        for i, q in enumerate(peers):
             remote(
-                ag_src.at[level, 1], ag_buf.at[level, ns - 1 - d],
-                ag_sem.at[level, 0], ag_sem.at[level, 1], {"space": peer(d)},
+                ag_src.at[level, 1], ag_buf.at[level, i],
+                ag_sem.at[level, 0], ag_sem.at[level, 1], {"space": q},
             ).start()
-            return c
-
-        lax.fori_loop(1, ns, send_total, 0)
 
     def sum_end(level):
         gram[pl.ds(s * piece, piece), :] = ag_src[level, 1]
         pltpu.make_async_copy(ag_buf.at[level], ag_buf.at[level], ag_sem.at[level, 1]).wait()
-        for i in range(ns - 1):
-            gram[pl.ds(peer(i + 1) * piece, piece), :] = ag_buf[level, i]
+        for i, q in enumerate(senders):
+            gram[pl.ds(q * piece, piece), :] = ag_buf[level, i]
         return gram[...]
 
     def side_of(level):
         return lax.rem(t // 2 ** (level - 1), 2)
+
+    ahead_side = side_of(AHEAD)
+    ahead_partner = {"tm": t + (1 - 2 * ahead_side) * 2 ** (AHEAD - 1)}
+
+    def ahead_exchange(joined):
+        keep = rows // 2**AHEAD
+        copy = remote(
+            joined.at[:, pl.ds((1 - ahead_side) * keep, keep)], ahead_rows.at[ahead_side],
+            ahead_sem.at[0], ahead_sem.at[1], ahead_partner,
+        )
+        copy.start()
+        ahead_rows[ahead_side] = joined[:, pl.ds(ahead_side * keep, keep), :]
+        sends.append(copy.wait_send)
+        return copy
+
+    def wide_start():
+        both = [jnp.concatenate([ahead_rows[i, 0], ahead_rows[i, 1]], axis=1) for i in range(2)]
+        wide_xp[...] = mm(both[0], both[1], TN).astype(BF16)
+        for i, q in enumerate(peers):
+            remote(
+                wide_xp.at[pl.ds(q * 2 * piece, 2 * piece)], wide_rs.at[i],
+                ahead_sem.at[2], ahead_sem.at[3], {"space": q},
+            ).start()
+
+    def wide_members():
+        pltpu.make_async_copy(wide_rs, wide_rs, ahead_sem.at[3]).wait()
+        total = wide_xp[pl.ds(s * 2 * piece, 2 * piece), :].astype(F32)
+        for i in range(ns - 1):
+            total = total + wide_rs[i].astype(F32)
+        wide_src[0] = total.astype(BF16)
+        size = 2**AHEAD
+
+        def send_member(d, c):
+            remote(
+                wide_src.at[0], wide_tm.at[size - 1 - d],
+                ahead_sem.at[4], ahead_sem.at[5], {"tm": member(AHEAD, d)},
+            ).start()
+            return c
+
+        lax.fori_loop(1, size, send_member, 0)
+
+    def wide_back():
+        pltpu.make_async_copy(wide_tm, wide_tm, ahead_sem.at[5]).wait()
+        total = wide_src[0].astype(F32)
+        for i in range(2**AHEAD - 1):
+            total = total + wide_tm[i].astype(F32)
+        wide_src[1] = (total * scale).astype(BF16)
+        for i, q in enumerate(peers):
+            remote(wide_src.at[1], wide_ag.at[i], ahead_sem.at[6], ahead_sem.at[7], {"space": q}).start()
+
+    def wide_end():
+        wide_gram[pl.ds(s * 2 * piece, 2 * piece), :] = wide_src[1]
+        pltpu.make_async_copy(wide_ag, wide_ag, ahead_sem.at[7]).wait()
+        for i, q in enumerate(senders):
+            wide_gram[pl.ds(q * 2 * piece, 2 * piece), :] = wide_ag[i]
+        return wide_gram[...].astype(F32)
+
+    def ahead_coefs_exchange(coef):
+        ahead_coefs[ahead_side] = coef
+        copy = remote(
+            ahead_coefs.at[ahead_side], ahead_coefs.at[ahead_side], ahead_sem.at[8], ahead_sem.at[9], ahead_partner
+        )
+        copy.start()
+        sends.append(copy.wait_send)
+        return copy
 
     sends = []
 
@@ -318,9 +391,25 @@
             for i in range(2):
                 ji[i] = mm(joined_energy[i], coefs[i], NT).astype(BF16)
             x = mm2(mm2(sum_end(1), coefs[1], NT).T, coefs[0], NT).T
+        elif level == AHEAD:
+            if level < levels:
+                gather(level - 1, offset)
+            siblings[level - 2].wait_recv()
+            store(level - 2)
+            coefs_copy.wait_recv()
+            for i in range(2):
+                left, right = ahead_coefs[i, :, :K], ahead_coefs[i, :, K:]
+                ji[i] = (mm(ahead_rows[i, 0], left, NT) + mm(ahead_rows[i, 1], right, NT)).astype(BF16)
+            x = around(ahead_coefs[0], wide_end(), ahead_coefs[1])
+            if level == levels:
+                modes_copy.wait_recv()
+                gather(level - 1, offset)
+            siblings[level - 1] = to_sibling(level - 1)
         else:
             image_copy.wait_recv()
             sum_start(level, mm(ji[0], ji[1], TN))
+            if level == AHEAD - 1:
+                rows_copy = ahead_exchange(ji)
             if level - 1 >= 1 and level < levels and split_of(level - 1) > 1:
                 gather(level - 1, offset)
             if level - 2 >= 1:
@@ -332,6 +421,9 @@
                 if split_of(level - 1) > 1:
                     gather(level - 1, offset)
             sum_back(level)
+            if level == AHEAD - 1:
+                rows_copy.wait_recv()
+                wide_start()
             x = sum_end(level)
             siblings[level - 1] = to_sibling(level - 1)
         st = sketch_t[level - 1]
@@ -342,14 +434,21 @@
         z1 = y1 + mm3(y0, x)
         y = jnp.concatenate([y0, y1], axis=1)
         z = jnp.concatenate([z0, z1], axis=1)
-        coef = factor_solve(mm3(y, z, NT), y).astype(BF16)
+        inner = mm3(y, z, NT)
+        if level == AHEAD - 1:
+            wide_members()
+        coef = factor_solve(inner, y).astype(BF16)
+        if level == AHEAD - 1:
+            coefs_copy = ahead_coefs_exchange(coef)
+            wide_back()
         c0, c1 = coef[:, :K], coef[:, K:]
         keep = rows // 2 ** split_of(level)
         if level <= CAP:
             offset = offset + side_of(level) * keep
         if level < levels:
-            image[level][...] = (mm(ji[0], c0, NT) + mm(ji[1], c1, NT)).astype(BF16)
-            image_copy = exchange(level + 1, image[level], 0, joined_image[level], im_sem)
+            if level != AHEAD - 1:
+                image[level][...] = (mm(ji[0], c0, NT) + mm(ji[1], c1, NT)).astype(BF16)
+                image_copy = exchange(level + 1, image[level], 0, joined_image[level], im_sem)
             modes_copy.wait_recv()
             target = gathered[level].at[slot_of(level)]
             target[pl.ds(offset, keep), :] = (mm(jm[0], c0, NT) + mm(jm[1], c1, NT)).astype(BF16)
@@ -383,7 +482,12 @@
     def _():
         down.wait_send()
 
+    pltpu.make_async_copy(wide_rs, wide_rs, ahead_sem.at[2]).wait()
+    pltpu.make_async_copy(wide_tm, wide_tm, ahead_sem.at[4]).wait()
+    pltpu.make_async_copy(wide_ag, wide_ag, ahead_sem.at[6]).wait()
     for level in range(levels + 1):
+        if level == AHEAD:
+            continue
         pltpu.make_async_copy(rs_buf.at[level], rs_buf.at[level], rs_sem.at[level, 0]).wait()
         if level:
             pltpu.make_async_copy(tm_buf[level], tm_buf[level], tm_sem.at[level, 0]).wait()
@@ -423,10 +527,19 @@
             pltpu.VMEM((count, ns - 1, piece, K), F32),
             pltpu.VMEM((K, K), F32),
             pltpu.VMEM((2, K, K), BF16),
+            pltpu.VMEM((2, 2, rows // 2**AHEAD, K), BF16),
+            pltpu.VMEM((2, K, 2 * K), BF16),
+            pltpu.VMEM((2 * K, 2 * K), BF16),
+            pltpu.VMEM((ns - 1, 2 * piece, 2 * K), BF16),
+            pltpu.VMEM((2**AHEAD - 1, 2 * piece, 2 * K), BF16),
+            pltpu.VMEM((2, 2 * piece, 2 * K), BF16),
+            pltpu.VMEM((ns - 1, 2 * piece, 2 * K), BF16),
+            pltpu.VMEM((2 * K, 2 * K), BF16),
             sems(4),
             sems(4),
             *[sems(count, 2)] * 7,
             sems(2),
+            sems(10),
             sems(count + 4),
         ],
         compiler_params=pltpu.CompilerParams(

time: 145 us -> 132 us (0.910)
  Pallas kernels: 139 us -> 127 us
    pallas_call x1, Pallas kernels: 139 us -> 127 us  [on_device(): pl.pallas_call(functools.partial(kernel, ns, levels), out_shape=jax.Shape...]
where the time goes in v4:
time: 132 us
  Pallas kernels  127 us (96%)
  local copies, waits for them, and re-layouts  5.37 us (4%)
    pallas_call x1, Pallas kernels, on_device(): pl.pallas_call(functools.partial(kernel, ns, levels), out_shape=jax.Shape...  127 us
    unnamed x9, local copies, waits for them, and re-layouts  5.37 us

profile of v4, /device:TPU:1, one launch (start us, length us, event | category | flops | bytes accessed | tf_op | source)
XLA Modules:
  0.0 132.0 jit_solution(3796511954931521768)
XLA Ops:
  0.0 0.0 copy-start
  0.0 1.5 %copy-done = bf16[8,7,128,128]{3,2,1,0:T(8,128)(2,1)S(1)} copy-done((bf16[8,7,128,128]{3,2,1,0:T(8,128)(2,1)S(1)}, bf16[8,7,128,128]{3,2,1,0:T(8,128)(2,1)}, u32[]{:S(2)}) %copy-start) | copy-done | bytes 1835032
  1.5 0.0 copy-start.1
  1.5 1.1 copy-done.1
  2.6 0.0 copy-start.2
  2.6 0.9 copy-done.2
  3.5 0.0 copy-start.3
  3.5 0.7 copy-done.3
  4.2 126.6 %shard_map.46 = bf16[6,1,1024,128]{3,2,1,0:T(8,128)(2,1)S(1)} custom-call(s32[8,7]{1,0:T(8,128)S(1)} %copy-done.3, bf16[1024,128]{1,0:T(8,128)(2,1)S(1)} %copy-done.2, bf16[8,7,128,128]{3,2,1,0:T(8,128)(2,1)S(1)} %copy-done, f32[5,256,128]{2,1,0:T(8,128)S(1)} %copy-done.1), custom_call_target="tpu_custom_call" | custom-call | tf_op jit(solution)/shard_map/pallas_call | solution.py:506
  130.8 1.1 copy.6
Async XLA Ops:
  0.0 1.5 %copy-start = (bf16[8,7,128,128]{3,2,1,0:T(8,128)(2,1)S(1)}, bf16[8,7,128,128]{3,2,1,0:T(8,128)(2,1)}, u32[]{:S(2)}) copy-start(bf16[8,7,128,128]{3,2,1,0:T(8,128)(2,1)} %energy_hbm.1) | copy-start | bytes 5505028
  1.5 1.1 copy-start.1
  2.6 0.9 copy-start.2
  3.5 0.7 copy-start.3

commit v5 on v4

--- a/solution.py
+++ b/solution.py
@@ -410,22 +410,24 @@
             sum_start(level, mm(ji[0], ji[1], TN))
             if level == AHEAD - 1:
                 rows_copy = ahead_exchange(ji)
+            modes_copy = start_modes()
             if level - 1 >= 1 and level < levels and split_of(level - 1) > 1:
                 gather(level - 1, offset)
             if level - 2 >= 1:
                 siblings[level - 2].wait_recv()
                 store(level - 2)
             sum_members(level)
+            sum_back(level)
             if level == levels:
                 modes_copy.wait_recv()
                 if split_of(level - 1) > 1:
                     gather(level - 1, offset)
-            sum_back(level)
             if level == AHEAD - 1:
                 rows_copy.wait_recv()
                 wide_start()
             x = sum_end(level)
-            siblings[level - 1] = to_sibling(level - 1)
+            if level < levels:
+                siblings[level - 1] = to_sibling(level - 1)
         st = sketch_t[level - 1]
         st0, st1 = st[:, :K], st[:, K:]
         y0 = st0 + mm3(st1, x, NT)
@@ -452,23 +454,31 @@
             modes_copy.wait_recv()
             target = gathered[level].at[slot_of(level)]
             target[pl.ds(offset, keep), :] = (mm(jm[0], c0, NT) + mm(jm[1], c1, NT)).astype(BF16)
-            if level < levels - 1:
-                modes_copy = exchange(level + 1, target, offset, joined_modes[level], mo_sem)
-            else:
+
+            def start_modes(level=level, target=target, start=offset, keep=keep):
+                if level < levels - 1:
+                    return exchange(level + 1, target, start, joined_modes[level], mo_sem)
                 side = side_of(levels)
-                chunk = target.at[pl.ds(offset, keep)]
-                modes_copy = remote(
+                chunk = target.at[pl.ds(start, keep)]
+                copy = remote(
                     chunk, chunk, mo_sem.at[levels, 0], mo_sem.at[levels, 1],
                     {"tm": t + (1 - 2 * side) * 2 ** (levels - 1)},
                 )
-                modes_copy.start()
-                sends.append(modes_copy.wait_send)
+                copy.start()
+                sends.append(copy.wait_send)
+                return copy
+
+            if level + 1 == AHEAD:
+                modes_copy = start_modes()
         else:
-            siblings[level - 1].wait_recv()
-            store(level - 1)
+            if level != AHEAD:
+                siblings[level - 1] = to_sibling(level - 1)
             pair = gathered[level - 1]
             for i in range(4):
-                part = slice(i * rows // 4, (i + 1) * rows // 4)
+                if i == 2:
+                    siblings[level - 1].wait_recv()
+                    store(level - 1)
+                part = pl.ds((core if i < 2 else 1 - core) * half + i % 2 * (half // 2), half // 2)
                 last_modes[part] = (mm(pair[0, part], c0, NT) + mm(pair[1, part], c1, NT)).astype(BF16)
                 copy = pltpu.make_async_copy(last_modes.at[part], out.at[level, 0, part], out_sem.at[level + i])
                 copy.start()

time: 132 us -> 129 us (0.977)
  Pallas kernels: 127 us -> 123 us
    pallas_call x1, Pallas kernels: 127 us -> 123 us  [on_device(): pl.pallas_call(functools.partial(kernel, ns, levels), out_shape=jax.Shape...]
where the time goes in v5:
time: 129 us; the launch traced here: 128 us
  Pallas kernels  123 us (95%)
  local copies, waits for them, and re-layouts  5.37 us (4%)
    pallas_call x1, Pallas kernels, on_device(): pl.pallas_call(functools.partial(kernel, ns, levels), out_shape=jax.Shape...  123 us
    unnamed x9, local copies, waits for them, and re-layouts  5.37 us

profile of v5, /device:TPU:1, one launch (start us, length us, event | category | flops | bytes accessed | tf_op | source)
XLA Modules:
  0.0 128.3 jit_solution(16440486377904271621)
XLA Ops:
  0.0 0.0 copy-start
  0.0 1.5 %copy-done = bf16[8,7,128,128]{3,2,1,0:T(8,128)(2,1)S(1)} copy-done((bf16[8,7,128,128]{3,2,1,0:T(8,128)(2,1)S(1)}, bf16[8,7,128,128]{3,2,1,0:T(8,128)(2,1)}, u32[]{:S(2)}) %copy-start) | copy-done | bytes 1835032
  1.5 0.0 copy-start.1
  1.5 1.1 copy-done.1
  2.6 0.0 copy-start.2
  2.6 0.9 copy-done.2
  3.5 0.0 copy-start.3
  3.5 0.7 copy-done.3
  4.2 123.0 %shard_map.46 = bf16[6,1,1024,128]{3,2,1,0:T(8,128)(2,1)S(1)} custom-call(s32[8,7]{1,0:T(8,128)S(1)} %copy-done.3, bf16[1024,128]{1,0:T(8,128)(2,1)S(1)} %copy-done.2, bf16[8,7,128,128]{3,2,1,0:T(8,128)(2,1)S(1)} %copy-done, f32[5,256,128]{2,1,0:T(8,128)S(1)} %copy-done.1), custom_call_target="tpu_custom_call" | custom-call | tf_op jit(solution)/shard_map/pallas_call | solution.py:516
  127.2 1.1 copy.6
Async XLA Ops:
  0.0 1.5 %copy-start = (bf16[8,7,128,128]{3,2,1,0:T(8,128)(2,1)S(1)}, bf16[8,7,128,128]{3,2,1,0:T(8,128)(2,1)}, u32[]{:S(2)}) copy-start(bf16[8,7,128,128]{3,2,1,0:T(8,128)(2,1)} %energy_hbm.1) | copy-start | bytes 5505028
  1.5 1.1 copy-start.1
  2.6 0.9 copy-start.2
  3.5 0.7 copy-start.3
